TPU v7x, 256 devices: a whole 4x4x8 slice. The times are simulated.
256 devices in a mesh: row: 32 (over y_hi, z, core), col: 8 (over x, y_lo).
Axes of the slice: x: 4, y: 4 (y_hi: 2, y_lo: 2; y = y_hi * 2 + y_lo), z: 8, core: 2. Of those that a mesh axis runs over, the one named last changes fastest.
Arguments:
- blocks: bfloat16 [320, 288, 128, 128], P('row', 'col')
- slot_cols: int32 [320, 288], P('row', 'col'), may hold values from 0 to 39, as said below
- counts: int32 [320, 8], P('row', 'col'), may hold values from 2 to 36, as said below
- demand: bfloat16 [40960, 128], P('col'), may hold values from 0.1 to 10
- value_added: float32 [40960], P('col'), may hold values from 0.5 to 5
Outputs:
- propagated: bfloat16 [40960, 128], P('row')
Inputs may be any that keep to these rules, and one draw needn't show every extreme that they name: `counts`: some block row has all 36 slots live in every column group; live slots come first in each group. `slot_cols`: within one block row and column group the 36 slots name distinct column blocks.
All inputs are finite; a program needn't handle non-finite values.
Results may differ from a plain program's by a relative error of at most 0.0042.
Values may be sent and summed in bfloat16 or wider, within the bound.
A program may use at most 128 MiB of HBM per device.

v0:
```python
import jax
import jax.numpy as jnp
from jax import lax
from jax.sharding import PartitionSpec as P


def body(blocks, slot_cols, counts, demand, value_added):
    rows_here = blocks.shape[0]
    slot_count = blocks.shape[1]
    block_size = blocks.shape[2]
    demand_width = demand.shape[1]
    group_blocks = demand.shape[0] // block_size
    live_slots = (jnp.arange(slot_count, dtype=jnp.int32)[None, :] < counts).astype(jnp.float32)
    column_sums = jnp.sum(blocks, axis=2, dtype=jnp.float32) * live_slots[:, :, None]
    onehot = (
        slot_cols.reshape(-1)[:, None] == jnp.arange(group_blocks, dtype=jnp.int32)[None, :]
    ).astype(jnp.float32)
    partial_totals = jnp.einsum(
        "nc,nk->ck", onehot, column_sums.reshape(-1, block_size), precision=lax.Precision.HIGHEST
    )
    totals = lax.psum(partial_totals, "row")
    inverse = 1.0 / (totals.reshape(-1) + value_added)
    inverse = inverse.reshape(group_blocks, block_size)
    scaling = inverse[slot_cols] * live_slots[:, :, None]
    coefficients = (blocks * scaling[:, :, None, :]).astype(jnp.bfloat16)

    def local_layer(source):
        picked = source.reshape(group_blocks, block_size, demand_width)[slot_cols]
        product = jnp.einsum(
            "bsij,bsjk->bik", coefficients, picked, preferred_element_type=jnp.float32
        )
        return product.reshape(rows_here * block_size, demand_width)

    group_index = lax.axis_index("col")
    group_rows = group_blocks * block_size
    part_one = local_layer(demand)
    layer_one = lax.psum(part_one, "col").astype(jnp.bfloat16)
    gathered = lax.all_gather(layer_one, "row", axis=0, tiled=True)
    needed = lax.dynamic_slice_in_dim(gathered, group_index * group_rows, group_rows, 0)
    layer_two = lax.psum(local_layer(needed), "col")
    return (layer_one.astype(jnp.float32) + layer_two).astype(jnp.bfloat16)


def solution(mesh):
    return jax.shard_map(
        body,
        mesh=mesh,
        in_specs=(
            P("row", "col", None, None),
            P("row", "col"),
            P("row", "col"),
            P("col", None),
            P("col"),
        ),
        out_specs=P("row", None),
        check_vma=False,
    )
```

profile of v0, /device:TPU:32, one launch (start us, length us, event | category | flops | bytes accessed | tf_op | source)
XLA Modules:
  0.0 431.5 jit_solution(1781961064499498028)
XLA Ops:
  6.5 0.0 copy-start
  6.5 0.0 copy-start.2
  6.5 0.0 all-gather.2.cloned.1.call-start
  6.5 0.9 eq.15
  7.4 0.7 compare_select_fusion
  8.1 0.7 fusion.8
  8.9 0.1 reshape.60
  8.9 0.1 reshape.63
  9.0 8.6 %convert_reduce_fusion = f32[10,36,128]{2,1,0:T(8,128)S(1)} fusion(bf16[10,36,128,128]{3,2,1,0:T(8,128)(2,1)} %param.5), kind=kLoop, calls=%fused_computation.4 | loop fusion | flops 11750400 | bytes 11980800 | tf_op jit(solution)/shard_map/reduce_sum | solution.py:14
  17.7 0.4 convolution_bitcast_fusion
  18.1 130.6 %psum.21 = f32[5120]{0:T(1024)S(1)} all-reduce(f32[5120]{0:T(1024)S(1)} %convolution_bitcast_fusion), channel_id=1, replica_groups=mesh['row'=32,'col'=8] {'row'}, use_global_device_ids=true, to_apply=%region_1.0 | all-reduce | flops 5120 | bytes 40960 | tf_op jit(solution)/shard_map/psum | solution.py:21
  148.7 0.0 copy-done.2
  148.7 1.1 gather_fusion
  149.9 0.1 broadcast_multiply_fusion
  150.0 0.0 copy-done
  150.0 11.1 %gather_fusion.1 = bf16[360,128,128]{2,1,0:T(8,128)(2,1)} fusion(bf16[40,128,128]{2,1,0:T(8,128)(2,1)S(1)} %bitcast.19, s32[1024]{0:T(1024)S(1)} %pad_clamp_fusion), kind=kCustom, calls=%fused_computation.1 | custom fusion | bytes 23594400 | tf_op jit(solution)/shard_map/gather | solution.py:28
  161.1 10.9 %fusion.3 = f32[10,128,128,1]{2,1,3,0:T(8,128)S(1)} fusion(bf16[10,36,128,128]{3,2,1,0:T(8,128)(2,1)} %bitcast.22, bf16[10,36,128,128]{3,2,1,0:T(8,128)(2,1)} %param.5, f32[10,36,128]{2,1,0:T(8,128)S(1)} %broadcast_multiply_fusion), kind=kOutput, calls=%fused_computation.7 | convolution fusion | flops 1527644160 | bytes 24432640 | tf_op jit(solution)/shard_map/bsij,bsjk->bik/dot_general | solution.py:29
  172.1 41.5 %all-reduce.4 = bf16[1280,128]{1,0:T(8,128)(2,1)} all-reduce(f32[1280,128]{1,0:T(8,128)S(1)} %bitcast.24), channel_id=1, replica_groups=mesh['row'=32,'col'=8] {'col'}, use_global_device_ids=true, to_apply=%region_2.0 | all-reduce | flops 163840 | bytes 983040 | tf_op jit(solution)/shard_map/psum | solution.py:37
  213.6 0.0 all-gather.2.cloned.1.call-update
  213.6 0.0 all-reduce.3.cloned.1.call-start
  213.6 107.5 %all-gather.2.cloned.1.call-done = bf16[40960,128]{1,0:T(8,128)(2,1)} async-done(((bf16[1280,128]{1,0:T(8,128)(2,1)}), bf16[40960,128]{1,0:T(8,128)(2,1)}) %all-gather.2.cloned.1.call-update) | async-done | bytes 10485776 | tf_op jit(solution)/shard_map/all_gather | solution.py:38
  321.1 1.4 constant_dynamic-slice_fusion
  322.5 11.1 %gather_fusion.2 = bf16[360,128,128]{2,1,0:T(8,128)(2,1)} fusion(bf16[40,128,128]{2,1,0:T(8,128)(2,1)S(1)} %bitcast.20, s32[1024]{0:T(1024)S(1)} %pad_clamp_fusion), kind=kCustom, calls=%fused_computation.2 | custom fusion | bytes 23594400 | tf_op jit(solution)/shard_map/gather | solution.py:28
  333.6 0.0 copy-start.1
  333.6 11.8 %fusion.1 = f32[10,128,128,1]{2,1,3,0:T(8,128)} fusion(bf16[10,36,128,128]{3,2,1,0:T(8,128)(2,1)} %bitcast.21, bf16[10,36,128,128]{3,2,1,0:T(8,128)(2,1)} %param.5, f32[10,36,128]{2,1,0:T(8,128)S(1)} %broadcast_multiply_fusion), kind=kOutput, calls=%fused_computation.6 | convolution fusion | flops 1527644160 | bytes 24432640 | tf_op jit(solution)/shard_map/bsij,bsjk->bik/dot_general | solution.py:29
  345.5 0.0 all-reduce.3.cloned.1.call-update
  345.5 77.3 %all-reduce.3.cloned.1.call-done = f32[1280,128]{1,0:T(8,128)} async-done(((f32[1280,128]{1,0:T(8,128)}), f32[1280,128]{1,0:T(8,128)}) %all-reduce.3.cloned.1.call-update) | async-done | bytes 655376 | tf_op jit(solution)/shard_map/psum | solution.py:40
  422.8 0.0 copy-done.1
  422.8 1.9 add_convert_fusion
  (4 shorter events, 0.0 us)
Async XLA Ops:
  6.5 143.5 %copy-start = (bf16[5120,128]{1,0:T(8,128)(2,1)S(1)}, bf16[5120,128]{1,0:T(8,128)(2,1)}, u32[]{:S(2)}) copy-start(bf16[5120,128]{1,0:T(8,128)(2,1)} %param.8) | copy-start | bytes 3932164
  6.5 142.2 %copy-start.2 = (f32[5120]{0:T(1024)S(1)}, f32[5120]{0:T(1024)}, u32[]{:S(2)}) copy-start(f32[5120]{0:T(1024)} %param.9) | copy-start | bytes 61444
  6.5 314.6 %all-gather.2.cloned.1.call-start = ((), (), s32[]{:S(2)}) async-start(), calls=%async_computation | async-start | bytes 10813440 | tf_op jit(solution)/shard_map/all_gather | solution.py:38
  213.6 209.2 %all-reduce.3.cloned.1.call-start = ((), (), s32[]{:S(2)}) async-start(), calls=%async_computation.1 | async-start | bytes 1310720 | tf_op jit(solution)/shard_map/psum | solution.py:40
  333.6 89.2 %copy-start.1 = (bf16[1280,128]{1,0:T(8,128)(2,1)S(1)}, bf16[1280,128]{1,0:T(8,128)(2,1)}, u32[]{:S(2)}) copy-start(bf16[1280,128]{1,0:T(8,128)(2,1)} %all-reduce.4) | copy-start | bytes 983044
Sparse Core Ops, SparseCore 0:
  213.7 107.3 all-gather.1
  345.6 77.1 all-reduce.2
where the time goes:
time: 432 us
  waiting for transfers between devices  185 us (43%)
  blocking collectives  172 us (40%)
  local copies, waits for them, and re-layouts  25.8 us (6%)
  matrix products  23.2 us (5%)
  between operations  13.5 us (3%)
  other arithmetic  12.1 us (3%)
    psum x1, blocking collectives, body(): totals = lax.psum(partial_totals, 'row')  131 us
    all_gather x1, waiting for transfers between devices, body(): gathered = lax.all_gather(layer_one, 'row', axis=0, tiled=True)  108 us
    psum x1, waiting for transfers between devices, body(): layer_two = lax.psum(local_layer(needed), 'col')  77.3 us
    psum x1, blocking collectives, body(): layer_one = lax.psum(part_one, 'col').astype(jnp.bfloat16)  41.5 us
    dot_general x2, matrix products, local_layer(): jnp.einsum('bsij,bsjk->bik', coefficients, picked, preferred_element_type...  22.8 us
    gather x2, local copies, waits for them, and re-layouts, local_layer(): picked = source.reshape(group_blocks, block_size, demand_width)[slot_cols]  22.2 us
  transfers between devices with their start and end apart: 2, of which 2 were waited for; matrix products, arithmetic and copies ran while one was open for 0% of the time, Pallas kernels for 0%

commit v1 on v0

--- a/solution.py
+++ b/solution.py
@@ -35,7 +35,9 @@
     group_rows = group_blocks * block_size
     part_one = local_layer(demand)
     layer_one = lax.psum(part_one, "col").astype(jnp.bfloat16)
-    gathered = lax.all_gather(layer_one, "row", axis=0, tiled=True)
+    gathered = jnp.concatenate(
+        lax.all_to_all(jnp.stack([layer_one] * lax.axis_size("row")), "row", 0, 0), axis=0
+    )
     needed = lax.dynamic_slice_in_dim(gathered, group_index * group_rows, group_rows, 0)
     layer_two = lax.psum(local_layer(needed), "col")
     return (layer_one.astype(jnp.float32) + layer_two).astype(jnp.bfloat16)

time: 432 us -> 575 us (1.33)
  waiting for transfers between devices: 185 us -> 312 us
  starting transfers between devices: 0.04 us -> 10.5 us
  local copies, waits for them, and re-layouts: 25.8 us -> 31.9 us
    all_to_all x0 -> x1, waiting for transfers between devices: none -> 229 us  [body(): lax.all_to_all(jnp.stack([layer_one] * lax.axis_size('row')), 'row', 0, 0)]
    all_gather x1 -> x0, waiting for transfers between devices: 108 us -> none  [body(): gathered = lax.all_gather(layer_one, 'row', axis=0, tiled=True)]
    all_to_all x0 -> x1, starting transfers between devices: none -> 10.5 us  [body(): lax.all_to_all(jnp.stack([layer_one] * lax.axis_size('row')), 'row', 0, 0)]
    another operation x0 -> x1, local copies, waits for them, and re-layouts: none -> 6.2 us  [body(): jnp.stack([layer_one] * lax.axis_size('row'))]
where the time goes in v1:
time: 575 us
  waiting for transfers between devices  312 us (54%)
  blocking collectives  172 us (30%)
  local copies, waits for them, and re-layouts  31.9 us (6%)
  matrix products  23.1 us (4%)
  between operations  13.5 us (2%)
  other arithmetic  12.2 us (2%)
  starting transfers between devices  10.5 us (2%)
    all_to_all x1, waiting for transfers between devices, body(): lax.all_to_all(jnp.stack([layer_one] * lax.axis_size('row')), 'row', 0, 0)  229 us
    psum x1, blocking collectives, body(): totals = lax.psum(partial_totals, 'row')  131 us
    psum x1, waiting for transfers between devices, body(): layer_two = lax.psum(local_layer(needed), 'col')  82.5 us
    psum x1, blocking collectives, body(): layer_one = lax.psum(part_one, 'col').astype(jnp.bfloat16)  40.9 us
    dot_general x2, matrix products, local_layer(): jnp.einsum('bsij,bsjk->bik', coefficients, picked, preferred_element_type...  22.7 us
    gather x2, local copies, waits for them, and re-layouts, local_layer(): picked = source.reshape(group_blocks, block_size, demand_width)[slot_cols]  22.2 us
  transfers between devices with their start and end apart: 2, of which 2 were waited for; matrix products, arithmetic and copies ran while one was open for 0% of the time, Pallas kernels for 0%

profile of v1, /device:TPU:32, one launch (start us, length us, event | category | flops | bytes accessed | tf_op | source)
XLA Modules:
  0.0 574.6 jit_solution(12891585133904517197)
XLA Ops:
  6.5 0.0 copy-start
  6.5 0.0 copy-start.1
  6.5 0.8 compare_select_fusion
  7.4 0.8 eq.15
  8.1 0.1 reshape.69
  8.2 0.7 fusion.8
  9.0 0.1 reshape.66
  9.0 8.6 %convert_reduce_fusion = f32[10,36,128]{2,1,0:T(8,128)S(1)} fusion(bf16[10,36,128,128]{3,2,1,0:T(8,128)(2,1)} %param.5), kind=kLoop, calls=%fused_computation.4 | loop fusion | flops 11750400 | bytes 11980800 | tf_op jit(solution)/shard_map/reduce_sum | solution.py:14
  17.7 0.4 convolution_bitcast_fusion
  18.1 130.6 %psum.21 = f32[5120]{0:T(1024)S(1)} all-reduce(f32[5120]{0:T(1024)S(1)} %convolution_bitcast_fusion), channel_id=1, replica_groups=mesh['row'=32,'col'=8] {'row'}, use_global_device_ids=true, to_apply=%region_1.0 | all-reduce | flops 5120 | bytes 40960 | tf_op jit(solution)/shard_map/psum | solution.py:21
  148.7 0.0 copy-done.1
  148.7 1.1 gather_fusion
  149.9 0.1 broadcast_multiply_fusion
  150.0 0.0 copy-done
  150.0 11.1 %gather_fusion.1 = bf16[360,128,128]{2,1,0:T(8,128)(2,1)} fusion(bf16[40,128,128]{2,1,0:T(8,128)(2,1)S(1)} %bitcast.20, s32[1024]{0:T(1024)S(1)} %pad_clamp_fusion), kind=kCustom, calls=%fused_computation.1 | custom fusion | bytes 23594400 | tf_op jit(solution)/shard_map/gather | solution.py:28
  161.1 10.9 %fusion.3 = f32[10,128,128,1]{2,1,3,0:T(8,128)S(1)} fusion(bf16[10,36,128,128]{3,2,1,0:T(8,128)(2,1)} %bitcast.23, bf16[10,36,128,128]{3,2,1,0:T(8,128)(2,1)} %param.5, f32[10,36,128]{2,1,0:T(8,128)S(1)} %broadcast_multiply_fusion), kind=kOutput, calls=%fused_computation.7 | convolution fusion | flops 1527644160 | bytes 24432640 | tf_op jit(solution)/shard_map/bsij,bsjk->bik/dot_general | solution.py:29
  172.1 40.9 %all-reduce.4 = bf16[1280,128]{1,0:T(8,128)(2,1)S(1)} all-reduce(f32[1280,128]{1,0:T(8,128)S(1)} %bitcast.25), channel_id=1, replica_groups=mesh['row'=32,'col'=8] {'col'}, use_global_device_ids=true, to_apply=%region_2.0 | all-reduce | flops 163840 | bytes 983040 | tf_op jit(solution)/shard_map/psum | solution.py:37
  213.0 6.2 %stack.2 = bf16[32,1280,128]{2,1,0:T(8,128)(2,1)} broadcast(bf16[1280,128]{1,0:T(8,128)(2,1)S(1)} %all-reduce.4), dimensions={1,2} | broadcast | bytes 10813440 | tf_op jit(solution)/shard_map/stack | solution.py:39
  219.2 10.5 %all-to-all-start = ((bf16[32,1280,128]{2,1,0:T(8,128)(2,1)}), bf16[32,1280,128]{2,1,0:T(8,128)(2,1)}, u32[]{:S(2)}, u32[]{:S(2)}) async-start(bf16[32,1280,128]{2,1,0:T(8,128)(2,1)} %stack.2), calls=%async_computation | async-start | bytes 20971520 | tf_op jit(solution)/shard_map/all_to_all | solution.py:39
  229.7 0.0 all-reduce.3.cloned.1.call-start
  229.8 229.2 %all-to-all-done = bf16[32,1280,128]{2,1,0:T(8,128)(2,1)} async-done(((bf16[32,1280,128]{2,1,0:T(8,128)(2,1)}), bf16[32,1280,128]{2,1,0:T(8,128)(2,1)}, u32[]{:S(2)}, u32[]{:S(2)}) %all-to-all-start) | async-done | bytes 10485792 | tf_op jit(solution)/shard_map/all_to_all | solution.py:39
  459.0 1.4 constant_dynamic-slice_fusion
  460.4 11.1 %gather_fusion.2 = bf16[360,128,128]{2,1,0:T(8,128)(2,1)} fusion(bf16[40,128,128]{2,1,0:T(8,128)(2,1)S(1)} %bitcast.21, s32[1024]{0:T(1024)S(1)} %pad_clamp_fusion), kind=kCustom, calls=%fused_computation.2 | custom fusion | bytes 23594400 | tf_op jit(solution)/shard_map/gather | solution.py:28
  471.5 11.8 %fusion.1 = f32[10,128,128,1]{2,1,3,0:T(8,128)} fusion(bf16[10,36,128,128]{3,2,1,0:T(8,128)(2,1)} %bitcast.22, bf16[10,36,128,128]{3,2,1,0:T(8,128)(2,1)} %param.5, f32[10,36,128]{2,1,0:T(8,128)S(1)} %broadcast_multiply_fusion), kind=kOutput, calls=%fused_computation.6 | convolution fusion | flops 1527644160 | bytes 24432640 | tf_op jit(solution)/shard_map/bsij,bsjk->bik/dot_general | solution.py:29
  483.3 0.0 all-reduce.3.cloned.1.call-update
  483.3 82.5 %all-reduce.3.cloned.1.call-done = f32[1280,128]{1,0:T(8,128)} async-done(((f32[1280,128]{1,0:T(8,128)}), f32[1280,128]{1,0:T(8,128)}) %all-reduce.3.cloned.1.call-update) | async-done | bytes 655376 | tf_op jit(solution)/shard_map/psum | solution.py:42
  565.9 1.9 add_convert_fusion
  (4 shorter events, 0.0 us)
Async XLA Ops:
  6.5 143.5 %copy-start = (bf16[5120,128]{1,0:T(8,128)(2,1)S(1)}, bf16[5120,128]{1,0:T(8,128)(2,1)}, u32[]{:S(2)}) copy-start(bf16[5120,128]{1,0:T(8,128)(2,1)} %param.8) | copy-start | bytes 3932164
  6.5 142.2 %copy-start.1 = (f32[5120]{0:T(1024)S(1)}, f32[5120]{0:T(1024)}, u32[]{:S(2)}) copy-start(f32[5120]{0:T(1024)} %param.9) | copy-start | bytes 61444
  219.2 239.8 %all-to-all-start = ((bf16[32,1280,128]{2,1,0:T(8,128)(2,1)}), bf16[32,1280,128]{2,1,0:T(8,128)(2,1)}, u32[]{:S(2)}, u32[]{:S(2)}) async-start(bf16[32,1280,128]{2,1,0:T(8,128)(2,1)} %stack.2), calls=%async_computation | async-start | bytes 20971520 | tf_op jit(solution)/shard_map/all_to_all | solution.py:39
  229.7 336.1 %all-reduce.3.cloned.1.call-start = ((), (), s32[]{:S(2)}) async-start(), calls=%async_computation.1 | async-start | bytes 1310720 | tf_op jit(solution)/shard_map/psum | solution.py:42
Sparse Core Ops, SparseCore 0:
  483.4 82.3 all-reduce.2

commit v2 on v0

--- a/solution.py
+++ b/solution.py
@@ -34,7 +34,7 @@
     group_index = lax.axis_index("col")
     group_rows = group_blocks * block_size
     part_one = local_layer(demand)
-    layer_one = lax.psum(part_one, "col").astype(jnp.bfloat16)
+    layer_one = jnp.sum(lax.all_gather(part_one, "col"), axis=0).astype(jnp.bfloat16)
     gathered = lax.all_gather(layer_one, "row", axis=0, tiled=True)
     needed = lax.dynamic_slice_in_dim(gathered, group_index * group_rows, group_rows, 0)
     layer_two = lax.psum(local_layer(needed), "col")

time: 432 us -> 509 us (1.18)
  waiting for transfers between devices: 185 us -> 299 us
  blocking collectives: 172 us -> 131 us
    all_gather x0 -> x1, waiting for transfers between devices: none -> 112 us  [body(): lax.all_gather(part_one, 'col')]
    psum x1 -> x0, blocking collectives: 41.5 us -> none  [body(): layer_one = lax.psum(part_one, 'col').astype(jnp.bfloat16)]
  transfers between devices with their start and end apart: 2 -> 3, of which waited for: 2 -> 3; matrix products, arithmetic and copies ran while one was open for 0% -> 0% of each run, Pallas kernels for 0% -> 0%
where the time goes in v2:
time: 509 us; the launch traced here: 508 us
  waiting for transfers between devices  299 us (59%)
  blocking collectives  131 us (26%)
  local copies, waits for them, and re-layouts  25.8 us (5%)
  matrix products  24 us (5%)
  other arithmetic  15.6 us (3%)
  between operations  13.2 us (3%)
    psum x1, blocking collectives, body(): totals = lax.psum(partial_totals, 'row')  131 us
    all_gather x1, waiting for transfers between devices, body(): lax.all_gather(part_one, 'col')  112 us
    all_gather x1, waiting for transfers between devices, body(): gathered = lax.all_gather(layer_one, 'row', axis=0, tiled=True)  110 us
    psum x1, waiting for transfers between devices, body(): layer_two = lax.psum(local_layer(needed), 'col')  77.3 us
    dot_general x2, matrix products, local_layer(): jnp.einsum('bsij,bsjk->bik', coefficients, picked, preferred_element_type...  23.6 us
    gather x2, local copies, waits for them, and re-layouts, local_layer(): picked = source.reshape(group_blocks, block_size, demand_width)[slot_cols]  22.2 us
  transfers between devices with their start and end apart: 3, of which 3 were waited for; matrix products, arithmetic and copies ran while one was open for 0% of the time, Pallas kernels for 0%

profile of v2, /device:TPU:32, one launch (start us, length us, event | category | flops | bytes accessed | tf_op | source)
XLA Modules:
  0.0 508.5 jit_solution(17588708712767172098)
XLA Ops:
  6.5 0.0 copy-start
  6.5 0.0 copy-start.2
  6.5 0.0 all-gather.3.cloned.1.call-start
  6.5 0.9 eq.15
  7.4 0.7 compare_select_fusion
  8.1 0.7 fusion.8
  8.9 0.1 reshape.56
  8.9 0.1 reshape.59
  9.0 8.6 %convert_reduce_fusion = f32[10,36,128]{2,1,0:T(8,128)S(1)} fusion(bf16[10,36,128,128]{3,2,1,0:T(8,128)(2,1)} %param.5), kind=kLoop, calls=%fused_computation.4 | loop fusion | flops 11750400 | bytes 11980800 | tf_op jit(solution)/shard_map/reduce_sum | solution.py:14
  17.7 0.4 convolution_bitcast_fusion
  18.1 130.6 %psum.14 = f32[5120]{0:T(1024)S(1)} all-reduce(f32[5120]{0:T(1024)S(1)} %convolution_bitcast_fusion), channel_id=1, replica_groups=mesh['row'=32,'col'=8] {'row'}, use_global_device_ids=true, to_apply=%region_1.0 | all-reduce | flops 5120 | bytes 40960 | tf_op jit(solution)/shard_map/psum | solution.py:21
  148.7 0.0 copy-done.2
  148.7 1.1 gather_fusion
  149.9 0.1 broadcast_multiply_fusion
  150.0 0.0 copy-done
  150.0 11.1 %gather_fusion.1 = bf16[360,128,128]{2,1,0:T(8,128)(2,1)} fusion(bf16[40,128,128]{2,1,0:T(8,128)(2,1)S(1)} %bitcast.19, s32[1024]{0:T(1024)S(1)} %pad_clamp_fusion), kind=kCustom, calls=%fused_computation.1 | custom fusion | bytes 23594400 | tf_op jit(solution)/shard_map/gather | solution.py:28
  161.1 11.8 %fusion.3 = f32[10,128,128,1]{2,1,3,0:T(8,128)} fusion(bf16[10,36,128,128]{3,2,1,0:T(8,128)(2,1)} %bitcast.22, bf16[10,36,128,128]{3,2,1,0:T(8,128)(2,1)} %param.5, f32[10,36,128]{2,1,0:T(8,128)S(1)} %broadcast_multiply_fusion), kind=kOutput, calls=%fused_computation.7 | convolution fusion | flops 1527644160 | bytes 24432640 | tf_op jit(solution)/shard_map/bsij,bsjk->bik/dot_general | solution.py:29
  172.9 0.0 all-gather.3.cloned.1.call-update
  172.9 0.2 all-gather.5.cloned.1.call-start
  173.2 111.6 %all-gather.3.cloned.1.call-done = f32[8,1280,128]{2,1,0:T(8,128)} async-done(((f32[1,1280,128]{2,1,0:T(8,128)}), f32[8,1280,128]{2,1,0:T(8,128)}) %all-gather.3.cloned.1.call-update) | async-done | bytes 5242896 | tf_op jit(solution)/shard_map/all_gather | solution.py:37
  284.7 3.6 reduce_sum.22
  288.3 0.0 all-gather.5.cloned.1.call-update
  288.3 0.0 all-reduce.2.cloned.1.call-start
  288.4 110.0 %all-gather.5.cloned.1.call-done = bf16[40960,128]{1,0:T(8,128)(2,1)} async-done(((bf16[1280,128]{1,0:T(8,128)(2,1)}), bf16[40960,128]{1,0:T(8,128)(2,1)}) %all-gather.5.cloned.1.call-update) | async-done | bytes 10485776 | tf_op jit(solution)/shard_map/all_gather | solution.py:38
  398.3 1.4 constant_dynamic-slice_fusion
  399.7 11.1 %gather_fusion.2 = bf16[360,128,128]{2,1,0:T(8,128)(2,1)} fusion(bf16[40,128,128]{2,1,0:T(8,128)(2,1)S(1)} %bitcast.20, s32[1024]{0:T(1024)S(1)} %pad_clamp_fusion), kind=kCustom, calls=%fused_computation.2 | custom fusion | bytes 23594400 | tf_op jit(solution)/shard_map/gather | solution.py:28
  410.9 0.0 copy-start.1
  410.9 11.8 %fusion.1 = f32[10,128,128,1]{2,1,3,0:T(8,128)} fusion(bf16[10,36,128,128]{3,2,1,0:T(8,128)(2,1)} %bitcast.21, bf16[10,36,128,128]{3,2,1,0:T(8,128)(2,1)} %param.5, f32[10,36,128]{2,1,0:T(8,128)S(1)} %broadcast_multiply_fusion), kind=kOutput, calls=%fused_computation.6 | convolution fusion | flops 1527644160 | bytes 24432640 | tf_op jit(solution)/shard_map/bsij,bsjk->bik/dot_general | solution.py:29
  422.7 0.0 all-reduce.2.cloned.1.call-update
  422.7 77.3 %all-reduce.2.cloned.1.call-done = f32[1280,128]{1,0:T(8,128)} async-done(((f32[1280,128]{1,0:T(8,128)}), f32[1280,128]{1,0:T(8,128)}) %all-reduce.2.cloned.1.call-update) | async-done | bytes 655376 | tf_op jit(solution)/shard_map/psum | solution.py:40
  500.1 0.0 copy-done.1
  500.1 1.9 add_convert_fusion
  (4 shorter events, 0.0 us)
Async XLA Ops:
  6.5 143.5 %copy-start = (bf16[5120,128]{1,0:T(8,128)(2,1)S(1)}, bf16[5120,128]{1,0:T(8,128)(2,1)}, u32[]{:S(2)}) copy-start(bf16[5120,128]{1,0:T(8,128)(2,1)} %param.8) | copy-start | bytes 3932164
  6.5 142.2 %copy-start.2 = (f32[5120]{0:T(1024)S(1)}, f32[5120]{0:T(1024)}, u32[]{:S(2)}) copy-start(f32[5120]{0:T(1024)} %param.9) | copy-start | bytes 61444
  6.5 278.2 %all-gather.3.cloned.1.call-start = ((), (), s32[]{:S(2)}) async-start(), calls=%async_computation | async-start | bytes 5898240 | tf_op jit(solution)/shard_map/all_gather | solution.py:37
  172.9 225.4 %all-gather.5.cloned.1.call-start = ((), (), s32[]{:S(2)}) async-start(), calls=%async_computation.1 | async-start | bytes 10813440 | tf_op jit(solution)/shard_map/all_gather | solution.py:38
  288.3 211.7 %all-reduce.2.cloned.1.call-start = ((), (), s32[]{:S(2)}) async-start(), calls=%async_computation.2 | async-start | bytes 1310720 | tf_op jit(solution)/shard_map/psum | solution.py:40
  410.9 89.2 %copy-start.1 = (bf16[1280,128]{1,0:T(8,128)(2,1)S(1)}, bf16[1280,128]{1,0:T(8,128)(2,1)}, u32[]{:S(2)}) copy-start(bf16[1280,128]{1,0:T(8,128)(2,1)} %reduce_sum.22) | copy-start | bytes 983044
Sparse Core Ops, SparseCore 0:
  173.1 111.6 all-gather.2
  288.4 109.8 all-gather.4
  422.8 77.1 all-reduce.1
